TPU v7x, 32 devices: a whole 2x2x4 slice. The times are simulated.
32 devices in a mesh: group: 1, expert: 32 (over z, y, x, core).
Axes of the slice: x: 2, y: 2, z: 4, core: 2. Of those that a mesh axis runs over, the one named last changes fastest.
Arguments:
- tokens: bfloat16 [4096, 3584], P(('group', 'expert')), may hold values from -6 to 6
- expert_ids: int32 [4096, 8], P(('group', 'expert')), may hold values from 0 to 31, as said below
- route_weight: float32 [4096, 8], P(('group', 'expert')), may hold values from 0.1 to 1
- expert_weight: bfloat16 [32, 3584, 1024], P('expert'), may hold values from -0.09375 to 0.09375
Outputs:
- routed: bfloat16 [4096, 8, 1024], P(('group', 'expert'))
Inputs may be any that keep to these rules, and one draw needn't show every extreme that they name: `expert_ids`: each token names 8 different experts; in every group one expert is named by exactly 48 rows of every device; every other expert is named by at most 32 rows of one device, and some expert reaches that.
All inputs are finite; a program needn't handle non-finite values.
Results may differ from a plain program's by a relative error of at most 0.005.
Values may be sent and summed in bfloat16 or wider, within the bound.
A program may use at most 128 MiB of HBM per device.

v0:
```python
import jax
import jax.numpy as jnp
from jax import lax
from jax.sharding import PartitionSpec as P


def body(tokens, expert_ids, route_weight, expert_weight):
    tok_rows, picks = expert_ids.shape
    per_device, model_width, hidden = expert_weight.shape
    devices = lax.axis_size("expert")
    experts = per_device * devices
    small_cap = (tok_rows * picks + experts - 1) // experts
    flat_ids = expert_ids.reshape(-1)
    columns = jnp.arange(experts, dtype=jnp.int32)
    onehot = (flat_ids[:, None] == columns[None, :]).astype(jnp.int32)
    capacity = max(small_cap + 1, small_cap + small_cap // 2)
    dispatched = jnp.ones_like(flat_ids)
    in_use = onehot * dispatched[:, None]
    before = jnp.cumsum(in_use, axis=0) - in_use
    ranking = jnp.sum(before * in_use, axis=1)
    slot_place = jnp.where(dispatched > 0, flat_ids * capacity + ranking, -1)
    positions = jnp.arange(experts * capacity, dtype=jnp.int32)
    chooser = jnp.sum(
        (slot_place.reshape(tok_rows, picks)[None, :, :] == positions[:, None, None]).astype(
            jnp.bfloat16
        ),
        axis=2,
    )
    packed = jnp.dot(chooser, tokens, preferred_element_type=jnp.float32).astype(jnp.bfloat16)
    packed = packed.reshape(experts, capacity, model_width)
    received = lax.all_to_all(packed, "expert", split_axis=0, concat_axis=0, tiled=True)
    slot_count = received.shape[1]
    grouped = received.reshape(devices, per_device, slot_count, model_width)
    preact = jnp.einsum(
        "necd,edf->necf", grouped, expert_weight, preferred_element_type=jnp.float32
    )
    activated = (
        jax.nn.silu(preact).astype(jnp.bfloat16).reshape(devices * per_device, slot_count, hidden)
    )
    results = lax.all_to_all(activated, "expert", split_axis=0, concat_axis=0, tiled=True)
    gathered = jnp.take(
        results.reshape(experts * capacity, hidden), jnp.maximum(slot_place, 0), axis=0
    )
    routed = route_weight.reshape(-1, 1) * gathered.astype(jnp.float32)
    return routed.astype(jnp.bfloat16).reshape(tok_rows, picks, hidden)


def solution(mesh):
    in_specs = (
        P(("group", "expert"), None),
        P(("group", "expert"), None),
        P(("group", "expert"), None),
        P("expert", None, None),
    )
    out_specs = P(("group", "expert"), None, None)
    return jax.shard_map(body, mesh=mesh, in_specs=in_specs, out_specs=out_specs, check_vma=False)
```

profile of v0, /device:TPU:7, one launch (start us, length us, event | category | flops | bytes accessed | tf_op | source)
XLA Modules:
  0.0 366.0 jit_solution(13075139223871415947)
XLA Ops:
  0.0 0.0 copy-start
  0.0 0.9 copy.22
  0.9 0.1 eq.39
  1.0 0.1 reshape.85
  1.1 9.0 %reduce-window.6 = s32[32,8,128]{2,1,0:T(8,128)S(1)} reduce-window(s32[32,8,128]{2,1,0:T(8,128)S(1)} %fusion.16, s32[]{:T(128)} %constant.28.clone.1), window={size=1x1x128 pad=0_0x0_0x127_0}, to_apply=%region_0.0 | reduce-window | flops 4161536 | bytes 262148 | tf_op jit(solution)/shard_map/reduce-window
  10.1 0.1 slice.10
  10.2 0.1 copy.24
  10.4 0.1 copy.25
  10.4 0.1 broadcast_add_fusion
  10.6 0.1 reduce_sum.26
  10.7 0.7 maximum_compare_fusion
  11.4 8.0 %fusion.9 = bf16[1536,128]{1,0:T(8,128)(2,1)S(1)} fusion(s32[128,8]{0,1:T(8,128)S(1)} %get-tuple-element.6), kind=kLoop, calls=%fused_computation.13 | loop fusion | flops 4521984 | bytes 397312 | tf_op jit(solution)/shard_map/reduce_sum | solution.py:23
  19.5 0.0 copy-done
  19.5 0.0 slice-start
  19.5 3.2 convolution_convert_fusion
  22.7 0.0 slice-start.1
  22.7 245.3 %all_to_all.10 = bf16[32,48,3584]{2,1,0:T(8,128)(2,1)S(1)} all-to-all(bf16[32,48,3584]{2,1,0:T(8,128)(2,1)S(1)} %bitcast.58), channel_id=1, replica_groups=mesh['group'=1,'expert'=32] {'expert'}, dimensions={0} | all-to-all | bytes 22020096 | tf_op jit(solution)/shard_map/all_to_all | solution.py:31
  268.1 0.0 slice-done
  268.1 0.0 slice-done.1
  268.1 13.6 %fusion.10 = bf16[32,48,1024]{2,1,0:T(8,128)(2,1)} fusion(bf16[32,48,3584]{2,1,0:T(8,128)(2,1)S(1)} %all_to_all.10, bf16[1,3584,1024]{2,1,0:T(8,128)(2,1)S(1)} %bitcast.64), kind=kOutput, calls=%fused_computation.15 | convolution fusion | flops 11282153472 | bytes 21495808 | tf_op jit(solution)/shard_map/necd,edf->necf/dot_general | solution.py:34
  281.6 0.0 copy-start.1
  281.6 0.0 copy-start.2
  281.6 4.6 %all-to-all-start.1 = ((bf16[32,48,1024]{2,1,0:T(8,128)(2,1)}), bf16[32,48,1024]{2,1,0:T(8,128)(2,1)}, u32[]{:S(2)}, u32[]{:S(2)}) async-start(bf16[32,48,1024]{2,1,0:T(8,128)(2,1)} %fusion.10), calls=%async_computation.1 | async-start | bytes 6291456 | tf_op jit(solution)/shard_map/all_to_all | solution.py:40
  286.2 0.0 copy-done.1
  286.3 0.1 copy.28
  286.4 0.1 mul.42
  286.5 0.1 copy.27
  286.6 0.0 copy-done.2
  286.6 0.1 copy.21
  286.7 70.1 %all-to-all-done.1 = bf16[32,48,1024]{2,1,0:T(8,128)(2,1)} async-done(((bf16[32,48,1024]{2,1,0:T(8,128)(2,1)}), bf16[32,48,1024]{2,1,0:T(8,128)(2,1)}, u32[]{:S(2)}, u32[]{:S(2)}) %all-to-all-start.1) | async-done | bytes 3145760 | tf_op jit(solution)/shard_map/all_to_all | solution.py:40
  356.8 7.3 %gather_fusion = bf16[1024,1024]{1,0:T(8,128)(2,1)S(1)} fusion(bf16[1536,1024]{1,0:T(8,128)(2,1)} %bitcast.11, s32[1024]{0:T(1024)S(1)} %broadcast_clamp_fusion), kind=kCustom, calls=%fused_computation | custom fusion | bytes 4198400 | tf_op jit(solution)/shard_map/jit(_take)/gather | solution.py:41
  364.1 1.9 multiply_convert_fusion
  (9 shorter events, 0.1 us)
Async XLA Ops:
  0.0 19.5 %copy-start = (bf16[128,3584]{1,0:T(8,128)(2,1)S(1)}, bf16[128,3584]{1,0:T(8,128)(2,1)}, u32[]{:S(2)}) copy-start(bf16[128,3584]{1,0:T(8,128)(2,1)} %param.4) | copy-start | bytes 2752516
  19.5 248.6 %slice-start = ((s8[7340032]{0:T(1024)(128)(4,1)}), s8[3145728]{0:T(1024)(128)(4,1)S(1)}, s32[]{:S(2)}) async-start(s8[7340032]{0:T(1024)(128)(4,1)} %bitcast.63), calls=%async_computation.2 | async-start | bytes 6291456
  22.7 245.4 %slice-start.1 = ((s8[7340032]{0:T(1024)(128)(4,1)}), s8[4194304]{0:T(1024)(128)(4,1)S(1)}, s32[]{:S(2)}) async-start(s8[7340032]{0:T(1024)(128)(4,1)} %bitcast.63), calls=%async_computation.3 | async-start | bytes 8388608
  281.6 4.6 %copy-start.1 = (s32[128,8]{0,1:T(8,128)S(1)}, s32[128,8]{0,1:T(8,128)}, u32[]{:S(2)}) copy-start(s32[128,8]{0,1:T(8,128)} %param.5) | copy-start | bytes 12292
  281.6 5.0 %copy-start.2 = (f32[128,8]{0,1:T(8,128)S(1)}, f32[128,8]{0,1:T(8,128)}, u32[]{:S(2)}) copy-start(f32[128,8]{0,1:T(8,128)} %param.6) | copy-start | bytes 12292
  281.6 75.2 %all-to-all-start.1 = ((bf16[32,48,1024]{2,1,0:T(8,128)(2,1)}), bf16[32,48,1024]{2,1,0:T(8,128)(2,1)}, u32[]{:S(2)}, u32[]{:S(2)}) async-start(bf16[32,48,1024]{2,1,0:T(8,128)(2,1)} %fusion.10), calls=%async_computation.1 | async-start | bytes 6291456 | tf_op jit(solution)/shard_map/all_to_all | solution.py:40
where the time goes:
time: 368 us; the launch traced here: 366 us
  blocking collectives  245 us (67%)
  waiting for transfers between devices  70.1 us (19%)
  other arithmetic  19.9 us (5%)
  matrix products  16.8 us (5%)
  local copies, waits for them, and re-layouts  9.2 us (2%)
  starting transfers between devices  4.6 us (1%)
    all_to_all x1, blocking collectives, body(): lax.all_to_all(packed, 'expert', split_axis=0, concat_axis=0, tiled=True)  245 us
    all_to_all x1, waiting for transfers between devices, body(): lax.all_to_all(activated, 'expert', split_axis=0, concat_axis=0, tiled=True)  70.1 us
    dot_general x1, matrix products, body(): jnp.einsum('necd,edf->necf', grouped, expert_weight, preferred_element_ty...  13.6 us
    another operation x3, other arithmetic  9.15 us
    reduce_sum x1, other arithmetic, body(): jnp.sum((slot_place.reshape(tok_rows, picks)[None, :, :] == positions[:,...  8.03 us
  transfers between devices with their start and end apart: 1, of which 1 were waited for; matrix products, arithmetic and copies ran while one was open for 0% of the time, Pallas kernels for 0%

commit v1 on v0

v1 whole, which is shorter than its diff:
```python
import jax
import jax.numpy as jnp
from jax import lax
from jax.experimental import pallas as pl
from jax.experimental.pallas import tpu as pltpu
from jax.sharding import PartitionSpec as P

MESH = pl.DeviceIdType.MESH
DEPTH = 4
PLANE = 8
COLS = 256


def slots(expert_ids, experts, capacity):
    columns = jnp.arange(experts, dtype=jnp.int32)
    named = expert_ids[:, :, None] == columns[None, None, :]
    mask = jnp.any(named, axis=1)
    rows = jnp.arange(expert_ids.shape[0], dtype=jnp.int32)
    earlier = (rows[None, :] < rows[:, None]).astype(jnp.bfloat16)
    rank = jnp.dot(earlier, mask.astype(jnp.bfloat16), preferred_element_type=jnp.float32)
    rank = rank.astype(jnp.int32)
    masked = jnp.where(mask, rank, -1)
    places = jnp.arange(capacity, dtype=jnp.int32)
    chooser = (masked.T[:, None, :] == places[None, :, None]).astype(jnp.bfloat16)
    picked = jnp.sum(jnp.where(named, rank[:, None, :], 0), axis=2)
    return chooser, expert_ids * capacity + picked


def exchange_kernel(
    tokens, chooser, weight, res, held, wv, selr, packed, outs,
    own_sem, w_sem, sel_send, sel_recv, send_sem, recv_sem, out_send, out_recv,
):
    me = lax.axis_index("expert")
    devices = held.shape[0]
    half = held.shape[1] // 2
    z = me // PLANE
    spot = lax.rem(me, PLANE)
    core = lax.rem(spot, 2)
    x = lax.rem(spot // 2, 2)
    y = spot // 4
    sib = me + 1 - 2 * core
    xn = me + 2 * (1 - 2 * x)
    yn = me + 4 * (1 - 2 * y)
    diag = 4 * (1 - 2 * y) + 2 * (1 - 2 * x)

    weight_copy = pltpu.make_async_copy(weight.at[0], wv, w_sem)
    weight_copy.start()
    own_copy = pltpu.make_async_copy(tokens, held.at[me], own_sem.at[0])
    own_copy.start()
    sel_copy = pltpu.make_async_copy(chooser.at[me], selr.at[me], own_sem.at[1])
    sel_copy.start()

    barrier = pltpu.get_barrier_semaphore()

    @pl.loop(1, devices)
    def _(d):
        pl.semaphore_signal(
            barrier, inc=1, device_id={"expert": lax.rem(me + d, devices)}, device_id_type=MESH
        )

    pl.semaphore_wait(barrier, devices - 1)
    own_copy.wait()
    sel_copy.wait()

    def sel_to(d):
        to = lax.rem(me + d, devices)
        return pltpu.make_async_remote_copy(
            src_ref=chooser.at[to], dst_ref=selr.at[me],
            send_sem=sel_send.at[to], recv_sem=sel_recv.at[me],
            device_id={"expert": to}, device_id_type=MESH,
        )

    def piece(block, h, to, index):
        part = held.at[block, pl.ds(h * half, half)]
        return pltpu.make_async_remote_copy(
            src_ref=part, dst_ref=part,
            send_sem=send_sem.at[index], recv_sem=recv_sem.at[block, h],
            device_id={"expert": to}, device_id_type=MESH,
        )

    sent = []

    def send(block, h, to, when=None):
        copy = piece(block, h, to, len(sent))
        if when is None:
            copy.start()
        else:
            pl.when(when)(copy.start)
        sent.append((copy, when))

    def arrived(block, h):
        piece(block, h, sib, 0).wait_recv()

    upper = z // 2
    mirrored = z + upper * (3 - 2 * z)

    def plane(t):
        order = t + mirrored * (1 - 2 * t) if t < 2 else t
        return order + upper * (3 - 2 * order)

    def base(t):
        return plane(t) * PLANE

    def stage_a(t):
        block, level = base(t) + spot, plane(t)
        for h in (0, 1):
            if t > 0:
                arrived(block, h)
            send(block, h, lax.rem(me + PLANE, devices),
                 jnp.logical_and(z < DEPTH - 1, level <= z))
            send(block, h, lax.rem(me + devices - PLANE, devices),
                 jnp.logical_and(z > 0, level >= z))
            send(block, h, (xn, yn)[h])
        for h in (0, 1):
            send(block, h, (yn, xn)[h])
            send(block, h, sib)

    def stage_b(t):
        for h, near, to in ((0, xn, yn), (1, yn, xn)):
            block = base(t) + lax.rem(near, PLANE)
            arrived(block, h)
            send(block, h, to)
            send(block, h, sib)

    def stage_c(t):
        across = base(t) + spot + diag
        for block, h in (
            (base(t) + lax.rem(yn, PLANE), 0), (base(t) + lax.rem(xn, PLANE), 1),
            (across, 0), (across, 1),
        ):
            arrived(block, h)
            send(block, h, sib)

    def out_to(s):
        return pltpu.make_async_remote_copy(
            src_ref=outs.at[s], dst_ref=res.at[me],
            send_sem=out_send.at[s], recv_sem=out_recv.at[me],
            device_id={"expert": s}, device_id_type=MESH,
        )

    cap = selr.shape[1]

    def stage_d(t):
        first = base(t)
        for q in range(4):
            for h in (0, 1):
                arrived(first + 2 * q + (1 - core), h)

        @pl.loop(0, PLANE)
        def _(q):
            s = first + q

            @pl.when(s != me)
            def _():
                pltpu.make_async_remote_copy(
                    src_ref=chooser.at[s], dst_ref=selr.at[s],
                    send_sem=sel_send.at[s], recv_sem=sel_recv.at[s],
                    device_id={"expert": sib}, device_id_type=MESH,
                ).wait_recv()

            rows = pl.ds(pl.multiple_of(q * cap, 16), cap)
            packed[rows, :] = jnp.dot(
                selr[s], held[s], preferred_element_type=jnp.float32
            ).astype(jnp.bfloat16)

        if t == 0:
            weight_copy.wait()

        @pl.loop(0, wv.shape[1] // COLS)
        def _(j):
            columns = pl.ds(pl.multiple_of(j * COLS, COLS), COLS)
            v = jnp.dot(packed[...], wv[:, columns], preferred_element_type=jnp.float32)
            act = (v / (1.0 + jnp.exp(-v))).astype(jnp.bfloat16)
            outs[pl.ds(first, PLANE), :, columns] = act.reshape(PLANE, cap, COLS)

        @pl.loop(0, PLANE)
        def _(q):
            s = first + q

            @pl.when(s != me)
            def _():
                out_to(s).start()

            @pl.when(s == me)
            def _():
                pltpu.make_async_copy(outs.at[me], res.at[me], own_sem.at[2]).start()

    stage_a(0)

    @pl.loop(1, devices)
    def _(d):
        sel_to(d).start()

    stage_b(0)
    stage_a(1)
    stage_c(0)
    stage_b(1)
    stage_a(2)
    stage_d(0)
    stage_c(1)
    stage_b(2)
    stage_a(3)
    stage_d(1)
    stage_c(2)
    stage_b(3)
    stage_d(2)
    stage_c(3)
    stage_d(3)

    for copy, when in sent:
        if when is None:
            copy.wait_send()
        else:
            pl.when(when)(copy.wait_send)

    @pl.loop(1, devices)
    def _(d):
        sel_to(d).wait_send()
        s = lax.rem(me + d, devices)
        out_to(s).wait_send()
        pltpu.make_async_remote_copy(
            src_ref=outs.at[s], dst_ref=res.at[s],
            send_sem=out_send.at[s], recv_sem=out_recv.at[s],
            device_id={"expert": s}, device_id_type=MESH,
        ).wait_recv()

    pltpu.make_async_copy(outs.at[me], res.at[me], own_sem.at[2]).wait()


def exchange(tokens, chooser, weight):
    rows, model_width = tokens.shape
    devices, capacity, _ = chooser.shape
    hidden = weight.shape[2]
    sends = 22 * DEPTH
    anywhere = pl.BlockSpec(memory_space=pl.ANY)
    return pl.pallas_call(
        exchange_kernel,
        out_shape=jax.ShapeDtypeStruct((devices, capacity, hidden), jnp.bfloat16),
        in_specs=[anywhere, pl.BlockSpec(memory_space=pltpu.VMEM), anywhere],
        out_specs=anywhere,
        scratch_shapes=[
            pltpu.VMEM((devices, rows, model_width), jnp.bfloat16),
            pltpu.VMEM((model_width, hidden), jnp.bfloat16),
            pltpu.VMEM((devices, capacity, rows), jnp.bfloat16),
            pltpu.VMEM((PLANE * capacity, model_width), jnp.bfloat16),
            pltpu.VMEM((devices, capacity, hidden), jnp.bfloat16),
            pltpu.SemaphoreType.DMA((3,)),
            pltpu.SemaphoreType.DMA,
            pltpu.SemaphoreType.DMA((devices,)),
            pltpu.SemaphoreType.DMA((devices,)),
            pltpu.SemaphoreType.DMA((sends,)),
            pltpu.SemaphoreType.DMA((devices, 2)),
            pltpu.SemaphoreType.DMA((devices,)),
            pltpu.SemaphoreType.DMA((devices,)),
        ],
        compiler_params=pltpu.CompilerParams(
            collective_id=0, has_side_effects=True, vmem_limit_bytes=56 * 1024 * 1024
        ),
    )(tokens, chooser, weight)


def body(tokens, expert_ids, route_weight, expert_weight):
    tok_rows, picks = expert_ids.shape
    per_device, model_width, hidden = expert_weight.shape
    devices = lax.axis_size("expert")
    experts = per_device * devices
    small_cap = (tok_rows * picks + experts - 1) // experts
    capacity = max(small_cap + 1, small_cap + small_cap // 2)
    chooser, place = slots(expert_ids, experts, capacity)
    if devices == DEPTH * PLANE and per_device == 1 and lax.axis_size("group") == 1:
        results = exchange(tokens, chooser, expert_weight)
    else:
        packed = jnp.dot(
            chooser.reshape(experts * capacity, tok_rows), tokens,
            preferred_element_type=jnp.float32,
        ).astype(jnp.bfloat16).reshape(experts, capacity, model_width)
        received = lax.all_to_all(packed, "expert", split_axis=0, concat_axis=0, tiled=True)
        grouped = received.reshape(devices, per_device, capacity, model_width)
        preact = jnp.einsum(
            "necd,edf->necf", grouped, expert_weight, preferred_element_type=jnp.float32
        )
        activated = jax.nn.silu(preact).astype(jnp.bfloat16).reshape(experts, capacity, hidden)
        results = lax.all_to_all(activated, "expert", split_axis=0, concat_axis=0, tiled=True)
    positions = jnp.arange(experts * capacity, dtype=jnp.int32)
    finder = (place.reshape(-1, 1) == positions[None, :]).astype(jnp.bfloat16)
    gathered = jnp.dot(
        finder, results.reshape(experts * capacity, hidden), preferred_element_type=jnp.float32
    )
    routed = route_weight.reshape(-1, 1) * gathered
    return routed.astype(jnp.bfloat16).reshape(tok_rows, picks, hidden)


def solution(mesh):
    in_specs = (
        P(("group", "expert"), None),
        P(("group", "expert"), None),
        P(("group", "expert"), None),
        P("expert", None, None),
    )
    out_specs = P(("group", "expert"), None, None)
    return jax.shard_map(body, mesh=mesh, in_specs=in_specs, out_specs=out_specs, check_vma=False)
```

time: 368 us -> 221 us (0.60)
  blocking collectives: 245 us -> 0 us
  Pallas kernels: 0 us -> 210 us
  waiting for transfers between devices: 70.1 us -> 0 us
  other arithmetic: 19.9 us -> 2.96 us
  matrix products: 16.8 us -> 6.93 us
  local copies, waits for them, and re-layouts: 9.2 us -> 1.08 us
  starting transfers between devices: 4.6 us -> 0 us
    all_to_all x1 -> x0, blocking collectives: 245 us -> none  [body(): lax.all_to_all(packed, 'expert', split_axis=0, concat_axis=0, tiled=True)]
    pallas_call x0 -> x1, Pallas kernels: none -> 210 us  [exchange(): pl.pallas_call(exchange_kernel, out_shape=jax.ShapeDtypeStruct((devices,...]
    all_to_all x1 -> x0, waiting for transfers between devices: 70.1 us -> none  [body(): lax.all_to_all(activated, 'expert', split_axis=0, concat_axis=0, tiled=True)]
    dot_general x2, matrix products: 16.8 us -> 6.93 us  [the longest x1 6.79 us: body(): jnp.dot(finder, results.reshape(experts * capacity, hidden), preferred_el...]
    another operation x3 -> x0, other arithmetic: 9.15 us -> none
    reduce_sum x2 -> x1, other arithmetic: 8.07 us -> 0.73 us  [slots(): picked = jnp.sum(jnp.where(named, rank[:, None, :], 0), axis=2)]
    gather x1 -> x0, local copies, waits for them, and re-layouts: 7.27 us -> none  [body(): jnp.take(results.reshape(experts * capacity, hidden), jnp.maximum(slot_pl...]
    all_to_all x1 -> x0, starting transfers between devices: 4.6 us -> none  [body(): lax.all_to_all(activated, 'expert', split_axis=0, concat_axis=0, tiled=True)]
  transfers between devices with their start and end apart: 1 -> 0, of which waited for: 1 -> 0; matrix products, arithmetic and copies ran while one was open for 0% -> 0% of each run, Pallas kernels for 0% -> 0%
where the time goes in v1:
time: 221 us
  Pallas kernels  210 us (95%)
  matrix products  6.93 us (3%)
  other arithmetic  2.96 us (1%)
    pallas_call x1, Pallas kernels, exchange(): pl.pallas_call(exchange_kernel, out_shape=jax.ShapeDtypeStruct((devices,...  210 us
    dot_general x1, matrix products, body(): jnp.dot(finder, results.reshape(experts * capacity, hidden), preferred_el...  6.79 us

profile of v1, /device:TPU:7, one launch (start us, length us, event | category | flops | bytes accessed | tf_op | source)
XLA Modules:
  0.0 220.9 jit_solution(11821293397231255226)
XLA Ops:
  0.0 0.7 fusion.4
  0.7 0.1 convolution_convert_fusion
  0.8 0.7 select_reduce_fusion
  1.6 0.7 multiply_add_fusion
  2.3 0.1 copy.12
  2.4 0.1 eq.44
  2.5 0.8 copy.11
  3.3 0.1 mul.16
  3.4 0.8 fusion.3.chooser
  4.2 209.9 %shard_map.46 = bf16[32,48,1024]{2,1,0:T(8,128)(2,1)} custom-call(bf16[128,3584]{1,0:T(8,128)(2,1)} %tokens.1, bf16[32,48,128]{2,1,0:T(8,128)(2,1)} %fusion.3.chooser, bf16[1,3584,1024]{2,1,0:T(8,128)(2,1)} %weight.1), custom_call_target="tpu_custom_call" | custom-call | tf_op jit(solution)/shard_map/pallas_call | solution.py:236
  214.1 6.8 %fusion.2 = bf16[128,8,1024]{2,1,0:T(8,128)(2,1)} fusion(f32[1024]{0:T(1024)S(1)} %mul.16, bf16[1536,1024]{1,0:T(8,128)(2,1)} %bitcast.7, s32[1024]{0:T(1024)S(1)} %eq.44), kind=kOutput, calls=%fused_computation.4 | convolution fusion | flops 3224895488 | bytes 5251072 | tf_op jit(solution)/shard_map/dot_general | solution.py:286
  (1 shorter events, 0.0 us)

commit v2 on v1

--- a/solution.py
+++ b/solution.py
@@ -173,9 +173,13 @@
             act = (v / (1.0 + jnp.exp(-v))).astype(jnp.bfloat16)
             outs[pl.ds(first, PLANE), :, columns] = act.reshape(PLANE, cap, COLS)
 
+
+    def send_out(t):
+        first = base(t)
+
         @pl.loop(0, PLANE)
         def _(q):
-            s = first + q
+            s = first + lax.rem(spot + q, PLANE)
 
             @pl.when(s != me)
             def _():
@@ -201,11 +205,15 @@
     stage_b(2)
     stage_a(3)
     stage_d(1)
+    send_out(1)
     stage_c(2)
     stage_b(3)
     stage_d(2)
+    send_out(2)
     stage_c(3)
     stage_d(3)
+    send_out(3)
+    send_out(0)
 
     for copy, when in sent:
         if when is None:

time: 221 us -> 204 us (0.923)
  Pallas kernels: 210 us -> 192 us
    pallas_call x1, Pallas kernels: 210 us -> 192 us  [exchange(): pl.pallas_call(exchange_kernel, out_shape=jax.ShapeDtypeStruct((devices,...]
where the time goes in v2:
time: 204 us; the launch traced here: 203 us
  Pallas kernels  192 us (94%)
  matrix products  6.93 us (3%)
  other arithmetic  2.96 us (1%)
    pallas_call x1, Pallas kernels, exchange(): pl.pallas_call(exchange_kernel, out_shape=jax.ShapeDtypeStruct((devices,...  192 us
    dot_general x1, matrix products, body(): jnp.dot(finder, results.reshape(experts * capacity, hidden), preferred_el...  6.79 us

profile of v2, /device:TPU:7, one launch (start us, length us, event | category | flops | bytes accessed | tf_op | source)
XLA Modules:
  0.0 203.2 jit_solution(1523511763859768815)
XLA Ops:
  0.0 0.7 fusion.4
  0.7 0.1 convolution_convert_fusion
  0.8 0.7 select_reduce_fusion
  1.6 0.7 multiply_add_fusion
  2.3 0.1 copy.12
  2.4 0.1 eq.44
  2.5 0.8 copy.11
  3.3 0.1 mul.16
  3.4 0.8 fusion.3.chooser
  4.2 192.2 %shard_map.46 = bf16[32,48,1024]{2,1,0:T(8,128)(2,1)} custom-call(bf16[128,3584]{1,0:T(8,128)(2,1)} %tokens.1, bf16[32,48,128]{2,1,0:T(8,128)(2,1)} %fusion.3.chooser, bf16[1,3584,1024]{2,1,0:T(8,128)(2,1)} %weight.1), custom_call_target="tpu_custom_call" | custom-call | tf_op jit(solution)/shard_map/pallas_call | solution.py:244
  196.5 6.8 %fusion.2 = bf16[128,8,1024]{2,1,0:T(8,128)(2,1)} fusion(f32[1024]{0:T(1024)S(1)} %mul.16, bf16[1536,1024]{1,0:T(8,128)(2,1)} %bitcast.7, s32[1024]{0:T(1024)S(1)} %eq.44), kind=kOutput, calls=%fused_computation.4 | convolution fusion | flops 3224895488 | bytes 5251072 | tf_op jit(solution)/shard_map/dot_general | solution.py:294
  (1 shorter events, 0.0 us)

commit v3 on v2

--- a/solution.py
+++ b/solution.py
@@ -163,7 +163,7 @@
                 selr[s], held[s], preferred_element_type=jnp.float32
             ).astype(jnp.bfloat16)
 
-        if t == 0:
+        if t == 1:
             weight_copy.wait()
 
         @pl.loop(0, wv.shape[1] // COLS)
@@ -200,16 +200,16 @@
     stage_c(0)
     stage_b(1)
     stage_a(2)
-    stage_d(0)
     stage_c(1)
     stage_b(2)
     stage_a(3)
     stage_d(1)
     send_out(1)
     stage_c(2)
-    stage_b(3)
     stage_d(2)
     send_out(2)
+    stage_b(3)
+    stage_d(0)
     stage_c(3)
     stage_d(3)
     send_out(3)

time: 204 us -> 200 us (0.980)
  Pallas kernels: 192 us -> 187 us
    pallas_call x1, Pallas kernels: 192 us -> 187 us  [exchange(): pl.pallas_call(exchange_kernel, out_shape=jax.ShapeDtypeStruct((devices,...]
where the time goes in v3:
time: 200 us; the launch traced here: 198 us
  Pallas kernels  187 us (94%)
  matrix products  6.93 us (3%)
  other arithmetic  2.96 us (1%)
    pallas_call x1, Pallas kernels, exchange(): pl.pallas_call(exchange_kernel, out_shape=jax.ShapeDtypeStruct((devices,...  187 us
    dot_general x1, matrix products, body(): jnp.dot(finder, results.reshape(experts * capacity, hidden), preferred_el...  6.79 us

profile of v3, /device:TPU:7, one launch (start us, length us, event | category | flops | bytes accessed | tf_op | source)
XLA Modules:
  0.0 198.0 jit_solution(6240715142853227018)
XLA Ops:
  0.0 0.7 fusion.4
  0.7 0.1 convolution_convert_fusion
  0.8 0.7 select_reduce_fusion
  1.6 0.7 multiply_add_fusion
  2.3 0.1 copy.12
  2.4 0.1 eq.44
  2.5 0.8 copy.11
  3.3 0.1 mul.16
  3.4 0.8 fusion.3.chooser
  4.2 187.0 %shard_map.46 = bf16[32,48,1024]{2,1,0:T(8,128)(2,1)} custom-call(bf16[128,3584]{1,0:T(8,128)(2,1)} %tokens.1, bf16[32,48,128]{2,1,0:T(8,128)(2,1)} %fusion.3.chooser, bf16[1,3584,1024]{2,1,0:T(8,128)(2,1)} %weight.1), custom_call_target="tpu_custom_call" | custom-call | tf_op jit(solution)/shard_map/pallas_call | solution.py:244
  191.2 6.8 %fusion.2 = bf16[128,8,1024]{2,1,0:T(8,128)(2,1)} fusion(f32[1024]{0:T(1024)S(1)} %mul.16, bf16[1536,1024]{1,0:T(8,128)(2,1)} %bitcast.7, s32[1024]{0:T(1024)S(1)} %eq.44), kind=kOutput, calls=%fused_computation.4 | convolution fusion | flops 3224895488 | bytes 5251072 | tf_op jit(solution)/shard_map/dot_general | solution.py:294
  (1 shorter events, 0.0 us)

commit v4 on v3

--- a/solution.py
+++ b/solution.py
@@ -197,11 +197,11 @@
 
     stage_b(0)
     stage_a(1)
+    stage_b(1)
     stage_c(0)
-    stage_b(1)
     stage_a(2)
+    stage_b(2)
     stage_c(1)
-    stage_b(2)
     stage_a(3)
     stage_d(1)
     send_out(1)

time: 200 us -> 200 us (level)
  no operation moved by 1% of the time
where the time goes in v4:
time: 200 us; the launch traced here: 198 us
  Pallas kernels  187 us (94%)
  matrix products  6.93 us (3%)
  other arithmetic  2.96 us (1%)
    pallas_call x1, Pallas kernels, exchange(): pl.pallas_call(exchange_kernel, out_shape=jax.ShapeDtypeStruct((devices,...  187 us
    dot_general x1, matrix products, body(): jnp.dot(finder, results.reshape(experts * capacity, hidden), preferred_el...  6.79 us

profile of v4, /device:TPU:7, one launch (start us, length us, event | category | flops | bytes accessed | tf_op | source)
XLA Modules:
  0.0 198.0 jit_solution(17746019290323594025)
XLA Ops:
  0.0 0.7 fusion.4
  0.7 0.1 convolution_convert_fusion
  0.8 0.7 select_reduce_fusion
  1.6 0.7 multiply_add_fusion
  2.3 0.1 copy.12
  2.4 0.1 eq.44
  2.5 0.8 copy.11
  3.3 0.1 mul.16
  3.4 0.8 fusion.3.chooser
  4.2 187.0 %shard_map.46 = bf16[32,48,1024]{2,1,0:T(8,128)(2,1)} custom-call(bf16[128,3584]{1,0:T(8,128)(2,1)} %tokens.1, bf16[32,48,128]{2,1,0:T(8,128)(2,1)} %fusion.3.chooser, bf16[1,3584,1024]{2,1,0:T(8,128)(2,1)} %weight.1), custom_call_target="tpu_custom_call" | custom-call | tf_op jit(solution)/shard_map/pallas_call | solution.py:244
  191.2 6.8 %fusion.2 = bf16[128,8,1024]{2,1,0:T(8,128)(2,1)} fusion(f32[1024]{0:T(1024)S(1)} %mul.16, bf16[1536,1024]{1,0:T(8,128)(2,1)} %bitcast.7, s32[1024]{0:T(1024)S(1)} %eq.44), kind=kOutput, calls=%fused_computation.4 | convolution fusion | flops 3224895488 | bytes 5251072 | tf_op jit(solution)/shard_map/dot_general | solution.py:294
  (1 shorter events, 0.0 us)
